TPU v7x, 32 devices: a whole 2x2x4 slice. The times are simulated.
32 devices in a mesh: exp: 8 (over z, y), grp: 4 (over x, core).
Axes of the slice: x: 2, y: 2, z: 4, core: 2. Of those that a mesh axis runs over, the one named last changes fastest.
Arguments:
- tiles: bfloat16 [128, 256, 256], P(('exp', 'grp')), may hold values from -6 to 6
- tile_exposure: int32 [128], P(('exp', 'grp')), may hold values from 0 to 63, as said below
- tile_patch: int32 [128, 4], P(('exp', 'grp')), may hold values from 0 to 7, all different within a row; in each aligned block of 4 rows (0 to 3, 4 to 7, ...) at most 2 rows name the same one
- tile_offset: int32 [128, 4, 2], P(('exp', 'grp')), may hold values from 0 to 256
- coeffs: bfloat16 [64, 10], P(('exp', 'grp')), may hold values from -2 to 2
- inv_var: bfloat16 [64], P(('exp', 'grp')), may hold values from 0.25 to 4
- vert_taps: bfloat16 [10, 41], replicated, may hold values from -1 to 1
- horiz_taps: bfloat16 [10, 41], replicated, may hold values from -1 to 1
Outputs:
- coadd: float32 [8, 512, 512], P('exp', 'grp')
Inputs may be any that keep to these rules, and one draw needn't show every extreme that they name: `tile_exposure`: each exposure is named by exactly 128 / 64 tiles. `tile_patch`: the entries of a row differ; among the rows of one device no patch is named by more than 2 rows. `tile_offset`: each tile lies wholly inside each patch listed for it.
All inputs are finite; a program needn't handle non-finite values.
Results may differ from a plain program's by a relative error of at most 0.0041.
Values may be sent and summed in bfloat16 or wider, within the bound.
A program may use at most 128 MiB of HBM per device.

v0:
```python
import math

import jax
import jax.numpy as jnp
from jax import lax
from jax.sharding import PartitionSpec as P

PS = 512


def band_matrix(filters, tile_side):
    terms, kernel_width = filters.shape
    half_width = (kernel_width - 1) // 2
    padding = tile_side - 1 - half_width
    padded = jnp.concatenate(
        [
            jnp.zeros((terms, padding), jnp.float32),
            filters.astype(jnp.float32),
            jnp.zeros((terms, padding + 1), jnp.float32),
        ],
        axis=1,
    )
    tiled = jnp.tile(padded, (1, tile_side + 1))[:, : tile_side * (2 * tile_side + 1)]
    window = tiled.reshape(terms, tile_side, 2 * tile_side + 1)[:, :, :tile_side]
    return window[:, ::-1, :].astype(jnp.bfloat16)


def coverage_rows(tags, row_count, tile_side, patch_side):
    weights = tags[:, 0].astype(jnp.float32)
    row_off = tags[:, 1].astype(jnp.int32)
    col_off = tags[:, 2].astype(jnp.int32)
    row_index = jnp.arange(row_count, dtype=jnp.int32)
    col_index = jnp.arange(patch_side, dtype=jnp.int32)
    row_mask = (
        (row_index[None, :] >= row_off[:, None])
        & (row_index[None, :] < row_off[:, None] + tile_side)
    ).astype(jnp.float32) * weights[:, None]
    col_mask = (
        (col_index[None, :] >= col_off[:, None])
        & (col_index[None, :] < col_off[:, None] + tile_side)
    ).astype(jnp.float32)
    return jnp.einsum("sy,sx->yx", row_mask, col_mask, precision=lax.Precision.HIGHEST)


def per_device(
    tiles, tile_exposure, tile_patch, tile_offset, coeffs, inv_var, vert_taps, horiz_taps
):
    n_owners = lax.axis_size("exp")
    tile_count = tiles.shape[0]
    tile_side = tiles.shape[1]
    listed = tile_patch.shape[1]
    entries = tile_count * listed
    capacity = max(2, (entries + n_owners - 1) // n_owners)
    slot_total = n_owners * capacity
    coef_all, weight_all = (
        lax.all_gather(coeffs, ("exp", "grp"), axis=0, tiled=True),
        lax.all_gather(inv_var, ("exp", "grp"), axis=0, tiled=True),
    )
    exposures = coef_all.shape[0]
    picker = (tile_exposure[:, None] == jnp.arange(exposures, dtype=jnp.int32)[None, :]).astype(
        jnp.bfloat16
    )
    coef_tile = jnp.dot(picker, coef_all, preferred_element_type=jnp.float32)
    weight_tile = jnp.dot(picker, weight_all[:, None], preferred_element_type=jnp.float32)[:, 0]
    vband = band_matrix(vert_taps, tile_side)
    hband = band_matrix(horiz_taps, tile_side)

    def convolve_one(inputs):
        one_tile, coef_row, weight = inputs
        rows_pass = jnp.einsum("yk,bxk->ybx", one_tile, hband, preferred_element_type=jnp.float32)
        partial_value = (rows_pass * coef_row[None, :, None]).astype(jnp.bfloat16)
        smoothed = jnp.einsum(
            "byk,kbx->yx", vband, partial_value, preferred_element_type=jnp.float32
        )
        return (weight * smoothed).astype(jnp.bfloat16)

    weighted = lax.map(convolve_one, (tiles, coef_tile, weight_tile))
    owners = tile_patch.reshape(entries)
    onehot = (owners[:, None] == jnp.arange(n_owners, dtype=jnp.int32)[None, :]).astype(jnp.int32)
    before = jnp.cumsum(onehot, axis=0) - onehot
    rank = jnp.sum(before * onehot, axis=1)
    target = owners * capacity + rank
    offsets = tile_offset.reshape(entries, 2)
    entry_tiles = jnp.repeat(weighted, listed, axis=0)
    entry_tags = jnp.stack(
        [
            jnp.repeat(weight_tile, listed),
            offsets[:, 0].astype(jnp.float32),
            offsets[:, 1].astype(jnp.float32),
        ],
        axis=1,
    ).astype(jnp.bfloat16)
    send_tiles = (
        jnp.zeros((slot_total, tile_side, tile_side), jnp.bfloat16).at[target].set(entry_tiles)
    )
    send_tags = jnp.zeros((slot_total, 3), jnp.bfloat16).at[target].set(entry_tags)
    got_tiles, got_tags = (
        lax.all_to_all(send_tiles, "exp", split_axis=0, concat_axis=0, tiled=True),
        lax.all_to_all(send_tags, "exp", split_axis=0, concat_axis=0, tiled=True),
    )
    got_rows = got_tags[:, 1].astype(jnp.int32)
    got_cols = got_tags[:, 2].astype(jnp.int32)
    block_slots = math.gcd(slot_total, 32)
    block_count = slot_total // block_slots
    inner = jnp.arange(tile_side, dtype=jnp.int32)
    col_index = jnp.arange(PS, dtype=jnp.int32)

    def place_block(canvas, inputs):
        block_tiles, block_rows, block_cols = inputs
        shifter = (
            col_index[None, None, :] == block_cols[:, None, None] + inner[None, :, None]
        ).astype(jnp.bfloat16)
        shifted = jnp.einsum(
            "syk,skx->syx", block_tiles, shifter, preferred_element_type=jnp.float32
        )
        row_index = (block_rows[:, None] + inner[None, :]).reshape(-1)
        canvas = canvas.at[row_index].add(shifted.reshape(-1, PS))
        return (canvas, None)

    flux, _ = lax.scan(
        place_block,
        jnp.zeros((PS, PS), jnp.float32),
        (
            got_tiles.reshape(block_count, block_slots, tile_side, tile_side),
            got_rows.reshape(block_count, block_slots),
            got_cols.reshape(block_count, block_slots),
        ),
    )
    cover = coverage_rows(got_tags, PS, tile_side, PS)
    flux_band, cover_band = (
        lax.psum_scatter(flux, "grp", scatter_dimension=0, tiled=True),
        lax.psum_scatter(cover, "grp", scatter_dimension=0, tiled=True),
    )
    coadd = flux_band / jnp.maximum(cover_band, 1.0)
    return coadd[None]


def solution(mesh):
    in_specs = (
        P(("exp", "grp"), None, None),
        P(("exp", "grp")),
        P(("exp", "grp"), None),
        P(("exp", "grp"), None, None),
        P(("exp", "grp"), None),
        P(("exp", "grp")),
        P(),
        P(),
    )
    out_specs = P("exp", "grp", None)
    return jax.shard_map(
        per_device, mesh=mesh, in_specs=in_specs, out_specs=out_specs, check_vma=False
    )
```

profile of v0, /device:TPU:0, one launch (start us, length us, event | category | flops | bytes accessed | tf_op | source)
XLA Modules:
  0.0 300.5 jit_solution(11796949780261311993)
XLA Ops:
  6.5 0.7 broadcast_multiply_fusion
  7.2 0.8 dynamic-update-slice
  8.1 0.8 eq.48
  8.8 42.0 %all-reduce = bf16[64]{0:T(256)(128)(2,1)S(1)} all-reduce(bf16[64]{0:T(256)(128)(2,1)S(1)} %dynamic-update-slice), channel_id=1, replica_groups=mesh['exp'=8,'grp'=4] {'exp','grp'}, use_global_device_ids=true, to_apply=%add | all-reduce | flops 64 | bytes 256
  50.8 0.8 fusion.41
  51.7 0.1 broadcast_in_dim.33
  51.7 0.1 stack_reshape.4
  51.8 0.7 copy.16
  52.5 0.1 reshape.137
  52.6 0.1 copy.17
  52.7 0.1 fusion.29
  52.8 0.2 select_reduce_fusion
  53.0 0.1 mul.47
  53.1 1.2 scatter_custom_fusion
  54.3 5.3 %all-to-all-start = ((bf16[8,2,3]{2,1,0:T(2,128)(2,1)}), bf16[8,2,3]{2,1,0:T(2,128)(2,1)S(1)}, u32[]{:S(2)}, u32[]{:S(2)}) async-start(bf16[8,2,3]{2,1,0:T(2,128)(2,1)} %bitcast.11), calls=%async_computation | async-start | bytes 8192 | tf_op jit(solution)/shard_map/all_to_all | solution.py:99
  59.6 0.1 pad.5.clone
  59.7 0.8 maximum_maximum_fusion.1
  60.5 0.2 tile.8
  60.7 0.3 pad.9
  61.0 1.6 copy.31
  62.5 2.1 slice.39
  64.6 8.3 %reshape.138 = bf16[10,256,513]{2,1,0:T(8,128)(2,1)S(1)} reshape(bf16[10,131328]{1,0:T(8,128)(2,1)} %slice.39) | data formatting | bytes 5253120 | tf_op jit(solution)/shard_map/reshape | solution.py:24
  73.0 1.2 slice.40
  74.1 19.4 %rev.6 = bf16[10,256,256]{2,1,0:T(8,128)(2,1)} reverse(bf16[10,256,256]{2,1,0:T(8,128)(2,1)} %slice.40), dimensions={1} | reverse | bytes 2621440 | tf_op jit(solution)/shard_map/rev | solution.py:25
  93.5 0.2 tile.20
  93.7 0.3 pad.10
  94.0 1.6 copy.32
  95.5 2.1 slice.41
  97.6 8.3 %reshape.139 = bf16[10,256,513]{2,1,0:T(8,128)(2,1)S(1)} reshape(bf16[10,131328]{1,0:T(8,128)(2,1)} %slice.41) | data formatting | bytes 5253120 | tf_op jit(solution)/shard_map/reshape | solution.py:24
  106.0 1.2 slice.42
  107.2 15.9 %rev.7 = bf16[10,256,256]{2,1,0:T(8,128)(2,1)S(1)} reverse(bf16[10,256,256]{2,1,0:T(8,128)(2,1)} %slice.42), dimensions={1} | reverse | bytes 2621440 | tf_op jit(solution)/shard_map/rev | solution.py:25
  123.1 40.8 %all-gather = bf16[32,2,10]{2,1,0:T(2,128)(2,1)S(1)} all-gather(bf16[1,2,10]{2,1,0:T(2,128)(2,1)S(1)} %bitcast.94), channel_id=1, replica_groups=mesh['exp'=8,'grp'=4] {'exp','grp'}, dimensions={0}, use_global_device_ids=true | all-gather | bytes 1320 | tf_op jit(solution)/shard_map/all_gather | solution.py:56
  163.9 0.2 fusion.30
  164.1 14.7 %while.2 = (s32[]{:T(128)}, bf16[4,256,256]{2,1,0:T(8,128)(2,1)S(1)}, f32[4]{0:T(128)S(1)}, bf16[4,256,256]{2,1,0:T(8,128)(2,1)}, bf16[10,256,256]{2,1,0:T(8,128...) while((s32[]{:T(128)}, bf16[4,256,256]{2,1,0:T(8,128)(2,1)S(1)}, ...), condition=%wide.region_4.5_spmd, body=%wide.region_3.4_spmd.sunk | while | flops 672530432 | bytes 3409121 | solution.py:77
  164.1 0.7 dynamic_slice.33
  164.8 2.9 fusion.55
  167.7 0.1 copy.34
  167.8 0.7 dynamic_slice.33
  168.5 2.9 fusion.55
  171.4 0.1 copy.34
  171.5 0.7 dynamic_slice.33
  172.2 2.9 fusion.55
  175.0 0.1 copy.34
  175.2 0.7 dynamic_slice.33
  175.9 2.9 fusion.55
  178.7 0.1 copy.34
  178.9 0.2 broadcast_in_dim.36
  179.1 1.6 broadcast_in_dim.34
  180.6 5.2 %scatter_fusion = bf16[16,256,256]{2,1,0:T(8,128)(2,1)} fusion(bf16[16,256,256]{2,1,0:T(8,128)(2,1)} %broadcast_in_dim.34, s32[16]{0:T(128)S(1)} %fusion.35, bf16[16,256,256]{2,1,0:T(8,128)(2,1)S(1)} %bitcast.89), kind=kCustom, calls=%fused_computation.1 | custom fusion | bytes 6291520 | tf_op jit(solution)/shard_map/scatter | solution.py:94
  185.9 3.6 %all-to-all-start.1 = ((bf16[16,256,256]{2,1,0:T(8,128)(2,1)}), bf16[16,256,256]{2,1,0:T(8,128)(2,1)S(1)}, u32[]{:S(2)}, u32[]{:S(2)}) async-start(bf16[16,256,256]{2,1,0:T(8,128)(2,1)} %scatter_fusion), calls=%async_computation.1 | async-start | bytes 4194304 | tf_op jit(solution)/shard_map/all_to_all | solution.py:98
  189.5 0.0 reduce-scatter.5.cloned.1.call-start
  189.5 0.1 fusion.40
  189.6 0.1 copy.27
  189.7 0.1 copy.28
  189.8 0.1 copy.29
  189.9 1.8 fusion.17
  191.7 0.0 reduce-scatter.3.cloned.1.call-start
  191.8 0.1 add_bitcast_fusion
  191.9 0.1 iota_add_fusion
  192.0 46.4 %all-to-all-done.1 = bf16[16,256,256]{2,1,0:T(8,128)(2,1)S(1)} async-done(((bf16[16,256,256]{2,1,0:T(8,128)(2,1)}), bf16[16,256,256]{2,1,0:T(8,128)(2,1)S(1)}, u32[]{:S(2)}, u32[]{:S(2)}) %all-to-all-start.1) | async-done | bytes 2097184 | tf_op jit(solution)/shard_map/all_to_all | solution.py:98
  238.4 4.1 %fusion.13 = f32[16,256,512]{2,1,0:T(8,128)} fusion(bf16[16,256,256]{2,1,0:T(8,128)(2,1)S(1)} %all-to-all-done.1, s32[16,256]{1,0:T(8,128)S(1)} %iota_add_fusion), kind=kOutput, calls=%fused_computation.17 | convolution fusion | flops 1075838976 | bytes 10502144 | tf_op jit(solution)/shard_map/while/body/eval_jaxpr/syk,skx->syx/dot_general | solution.py:113
  242.5 26.2 %scatter_custom_fusion.2 = f32[512,512]{1,0:T(8,128)} fusion(s32[4096]{0:T(1024)S(1)} %bitcast.92, f32[4096,512]{1,0:T(8,128)} %bitcast.84, f32[]{:T(128)} %constant.20.clone.1), kind=kCustom, calls=%fused_computation.20 | custom fusion | flops 2097152 | bytes 1049088 | tf_op jit(solution)/shard_map/while/body/eval_jaxpr/scatter-add | solution.py:117
  268.7 23.1 %reduce-scatter.3.cloned.1.call-done = f32[128,512]{1,0:T(8,128)} async-done(((f32[512,512]{1,0:T(8,128)}), f32[128,512]{1,0:T(8,128)}) %reduce-scatter.3.cloned.1.call-update) | async-done | bytes 262160 | tf_op jit(solution)/shard_map/reduce_scatter | solution.py:131
  291.8 1.8 divide_bitcast_fusion
  (34 shorter events, 0.3 us)
Async XLA Ops:
  54.3 131.6 %all-to-all-start = ((bf16[8,2,3]{2,1,0:T(2,128)(2,1)}), bf16[8,2,3]{2,1,0:T(2,128)(2,1)S(1)}, u32[]{:S(2)}, u32[]{:S(2)}) async-start(bf16[8,2,3]{2,1,0:T(2,128)(2,1)} %bitcast.11), calls=%async_computation | async-start | bytes 8192 | tf_op jit(solution)/shard_map/all_to_all | solution.py:99
  106.0 17.1 %copy-start.2 = (bf16[2,10]{1,0:T(2,128)(2,1)S(1)}, bf16[2,10]{1,0:T(2,128)(2,1)}, u32[]{:S(2)}) copy-start(bf16[2,10]{1,0:T(2,128)(2,1)} %param.14) | copy-start | bytes 124
  106.0 58.0 %copy-start.3 = (s32[4]{0:T(128)S(1)}, s32[4]{0:T(128)}, u32[]{:S(2)}) copy-start(s32[4]{0:T(128)} %param.11) | copy-start | bytes 52
  107.2 57.0 %copy-start = (bf16[10,256,256]{2,1,0:T(8,128)(2,1)S(1)}, bf16[10,256,256]{2,1,0:T(8,128)(2,1)}, u32[]{:S(2)}) copy-start(bf16[10,256,256]{2,1,0:T(8,128)(2,1)} %rev.6) | copy-start | bytes 3932164
  107.2 57.0 %copy-start.1 = (bf16[4,256,256]{2,1,0:T(8,128)(2,1)S(1)}, bf16[4,256,256]{2,1,0:T(8,128)(2,1)}, u32[]{:S(2)}) copy-start(bf16[4,256,256]{2,1,0:T(8,128)(2,1)} %custom-call) | copy-start | bytes 1572868
  185.9 52.5 %all-to-all-start.1 = ((bf16[16,256,256]{2,1,0:T(8,128)(2,1)}), bf16[16,256,256]{2,1,0:T(8,128)(2,1)S(1)}, u32[]{:S(2)}, u32[]{:S(2)}) async-start(bf16[16,256,256]{2,1,0:T(8,128)(2,1)} %scatter_fusion), calls=%async_computation.1 | async-start | bytes 4194304 | tf_op jit(solution)/shard_map/all_to_all | solution.py:98
  189.5 79.2 %reduce-scatter.5.cloned.1.call-start = ((), (), s32[]{:S(2)}) async-start(), calls=%async_computation.5 | async-start | bytes 1310720 | tf_op jit(solution)/shard_map/reduce_scatter | solution.py:132
  191.7 100.1 %reduce-scatter.3.cloned.1.call-start = ((), (), s32[]{:S(2)}) async-start(), calls=%async_computation.4 | async-start | bytes 1310720 | tf_op jit(solution)/shard_map/reduce_scatter | solution.py:131
Sparse Core Ops, SparseCore 0:
  192.9 25.3 reduce-scatter.4
  268.8 22.9 reduce-scatter.2
where the time goes:
time: 305 us; the launch traced here: 300 us
  blocking collectives  82.8 us (27%)
  local copies, waits for them, and re-layouts  77.1 us (25%)
  waiting for transfers between devices  69.6 us (23%)
  other arithmetic  29.9 us (10%)
  matrix products  18.4 us (6%)
  between operations  13.6 us (4%)
  starting transfers between devices  8.99 us (3%)
    all_to_all x1, waiting for transfers between devices, per_device(): lax.all_to_all(send_tiles, 'exp', split_axis=0, concat_axis=0, tiled=True)  46.4 us
    unnamed x1, blocking collectives  42 us
    all_gather x1, blocking collectives, per_device(): lax.all_gather(coeffs, ('exp', 'grp'), axis=0, tiled=True)  40.8 us
    rev x2, local copies, waits for them, and re-layouts, band_matrix(): return window[:, ::-1, :].astype(jnp.bfloat16)  35.3 us
    scatter-add x1, other arithmetic, place_block(): canvas = canvas.at[row_index].add(shifted.reshape(-1, PS))  26.2 us
    reduce_scatter x1, waiting for transfers between devices, per_device(): lax.psum_scatter(flux, 'grp', scatter_dimension=0, tiled=True)  23.1 us
    reshape x2, local copies, waits for them, and re-layouts, band_matrix(): tiled.reshape(terms, tile_side, 2 * tile_side + 1)[:, :, :tile_side]  16.7 us
    dot_general x4, matrix products, convolve_one(): jnp.einsum('byk,kbx->yx', vband, partial_value, preferred_element_type=jn...  11.4 us
  transfers between devices with their start and end apart: 4, of which 2 were waited for; matrix products, arithmetic and copies ran while one was open for 39% of the time, Pallas kernels for 0%

commit v1 on v0

v1 whole, which is shorter than its diff:
```python
import functools

import jax
import jax.numpy as jnp
from jax import lax
from jax.experimental import pallas as pl
from jax.experimental.pallas import tpu as pltpu
from jax.sharding import PartitionSpec as P

PS = 512
MESH = pl.DeviceIdType.MESH
VMEM = pl.BlockSpec(memory_space=pltpu.VMEM)
SMEM = pl.BlockSpec(memory_space=pltpu.SMEM)


def gather_kernel(n_exp, n_grp, block_ref, out_ref, held, send_a, recv_a, send_b, recv_b):
    e = lax.axis_index("exp")
    g = lax.axis_index("grp")
    barrier = pltpu.get_barrier_semaphore()
    for i in range(1, n_grp):
        pl.semaphore_signal(
            barrier, inc=1, device_id=(e, lax.rem(g + i, n_grp)), device_id_type=MESH
        )
    for i in range(1, n_exp):
        pl.semaphore_signal(
            barrier, inc=1, device_id=(lax.rem(e + i, n_exp), g), device_id_type=MESH
        )
    pl.semaphore_wait(barrier, n_grp + n_exp - 2)

    held[e, g] = block_ref[...]
    copies = []
    for i in range(1, n_grp):
        copy = pltpu.make_async_remote_copy(
            src_ref=block_ref,
            dst_ref=held.at[e, g],
            send_sem=send_a.at[i - 1],
            recv_sem=recv_a.at[i - 1],
            device_id=(e, lax.rem(g + i, n_grp)),
            device_id_type=MESH,
        )
        copy.start()
        copies.append(copy)
    for copy in copies:
        copy.wait()
    copies = []
    for i in range(1, n_exp):
        copy = pltpu.make_async_remote_copy(
            src_ref=held.at[e],
            dst_ref=held.at[e],
            send_sem=send_b.at[i - 1],
            recv_sem=recv_b.at[i - 1],
            device_id=(lax.rem(e + i, n_exp), g),
            device_id_type=MESH,
        )
        copy.start()
        copies.append(copy)
    for copy in copies:
        copy.wait()
    out_ref[...] = held[...]


def gather_blocks(block, n_exp, n_grp):
    shape = (n_exp, n_grp) + block.shape
    return pl.pallas_call(
        functools.partial(gather_kernel, n_exp, n_grp),
        out_shape=jax.ShapeDtypeStruct(shape, block.dtype),
        in_specs=[VMEM],
        out_specs=VMEM,
        scratch_shapes=[
            pltpu.VMEM(shape, block.dtype),
            pltpu.SemaphoreType.DMA((n_grp - 1,)),
            pltpu.SemaphoreType.DMA((n_grp - 1,)),
            pltpu.SemaphoreType.DMA((n_exp - 1,)),
            pltpu.SemaphoreType.DMA((n_exp - 1,)),
        ],
        compiler_params=pltpu.CompilerParams(collective_id=0, has_side_effects=True),
    )(block)


def canvas_kernel(
    half, patch_ref, row_ref, col_ref, coef_ref, weight_ref, tiles_ref, vtap_ref, htap_ref,
    out_ref, vband, hband, weighted,
):
    terms, side = vtap_ref.shape
    count = tiles_ref.shape[0]
    listed = patch_ref.shape[0] // count
    patch = pl.program_id(0)

    @pl.when(patch == 0)
    def _():
        row = lax.broadcasted_iota(jnp.int32, (side, side), 0)
        col = lax.broadcasted_iota(jnp.int32, (side, side), 1)
        inside = jnp.abs(col - row) <= half

        def build(b, carry):
            for taps, band in ((vtap_ref, vband), (htap_ref, hband)):
                line = jnp.broadcast_to(taps[pl.ds(b, 1), :], (side, side))
                line = pltpu.roll(line, side - half // 8 * 8, 1, stride=1, stride_axis=0)
                band[b] = jnp.where(inside, line, 0.0).astype(jnp.bfloat16)
            return carry

        lax.fori_loop(0, terms, build, 0)

        def convolve(t, carry):
            tile = tiles_ref[t]
            total = jnp.zeros((side, side), jnp.float32)
            for b in range(terms):
                across = jnp.dot(tile, hband[b], preferred_element_type=jnp.float32)
                part = (across * coef_ref[t * terms + b]).astype(jnp.bfloat16)
                total += jnp.dot(vband[b], part, preferred_element_type=jnp.float32)
            weighted[t] = (weight_ref[t] * total).astype(jnp.bfloat16)
            return carry

        lax.fori_loop(0, count, convolve, 0)

    far = -4 * PS
    picked = [[jnp.int32(0), jnp.int32(far), jnp.int32(far)] for _ in range(2)]
    found = jnp.int32(0)
    for t in range(count):
        for j in range(listed):
            n = t * listed + j
            hit = patch_ref[n] == patch
            for slot in range(2):
                take = hit & (found == slot)
                picked[slot] = [
                    jnp.where(take, new, old)
                    for new, old in zip((t, row_ref[n], col_ref[n]), picked[slot])
                ]
            found = found + hit.astype(jnp.int32)

    inner_c = lax.broadcasted_iota(jnp.int32, (side, PS), 1) - lax.broadcasted_iota(
        jnp.int32, (side, PS), 0
    )
    inner_r = lax.broadcasted_iota(jnp.int32, (PS, side), 0) - lax.broadcasted_iota(
        jnp.int32, (PS, side), 1
    )
    canvas = jnp.zeros((PS, PS), jnp.float32)
    for t, row_off, col_off in picked:
        col_pick = jnp.where(inner_c == col_off, 1.0, 0.0).astype(jnp.bfloat16)
        row_pick = jnp.where(inner_r == row_off, 1.0, 0.0).astype(jnp.bfloat16)
        moved = jnp.dot(weighted[t], col_pick, preferred_element_type=jnp.float32)
        canvas += jnp.dot(
            row_pick, moved.astype(jnp.bfloat16), preferred_element_type=jnp.float32
        )
    out_ref[0] = canvas.astype(jnp.bfloat16)


def local_canvases(patches, tile_patch, tile_offset, coef_tile, weight_tile, tiles, vtaps, htaps):
    count, side, _ = tiles.shape
    terms, width = vtaps.shape
    half = (width - 1) // 2
    pad = ((0, 0), (0, side - width))
    vline = jnp.roll(jnp.pad(vtaps.astype(jnp.float32), pad), -(half % 8), axis=1)
    hline = jnp.roll(jnp.pad(htaps.astype(jnp.float32)[:, ::-1], pad), -(half % 8), axis=1)
    return pl.pallas_call(
        functools.partial(canvas_kernel, half),
        grid=(patches,),
        out_shape=jax.ShapeDtypeStruct((patches, PS, PS), jnp.bfloat16),
        in_specs=[SMEM] * 5 + [VMEM] * 3,
        out_specs=pl.BlockSpec((1, PS, PS), lambda p: (p, 0, 0)),
        scratch_shapes=[
            pltpu.VMEM((terms, side, side), jnp.bfloat16),
            pltpu.VMEM((terms, side, side), jnp.bfloat16),
            pltpu.VMEM((count, side, side), jnp.bfloat16),
        ],
        compiler_params=pltpu.CompilerParams(vmem_limit_bytes=40 << 20),
    )(
        tile_patch.reshape(-1),
        tile_offset[:, :, 0].reshape(-1),
        tile_offset[:, :, 1].reshape(-1),
        coef_tile.reshape(-1),
        weight_tile,
        tiles,
        vline,
        hline,
    )


def reduce_kernel(
    steps, canvas, out_ref, got1, sum1, got2, sum2, got3, sum3, got4, sends, recvs
):
    e = lax.axis_index("exp")
    g = lax.axis_index("grp")
    hi, lo = e // 2, lax.rem(e, 2)
    far, near = g // 2, lax.rem(g, 2)
    by_core = (e, 2 * far + 1 - near)
    by_x = (e, 2 * (1 - far) + near)
    by_y = (2 * hi + 1 - lo, g)
    goal = [lax.rem(hi + 1 + k, steps) for k in range(steps)]
    by_z = [(2 * goal[k] + lo, g) for k in range(steps - 1)]

    barrier = pltpu.get_barrier_semaphore()
    for partner in [by_core, by_x, by_y] + by_z:
        pl.semaphore_signal(barrier, inc=1, device_id=partner, device_id_type=MESH)
    pl.semaphore_wait(barrier, steps + 2)

    def send(stage, k, src, dst, partner):
        copy = pltpu.make_async_remote_copy(
            src_ref=src,
            dst_ref=dst,
            send_sem=sends.at[stage, k],
            recv_sem=recvs.at[stage, k],
            device_id=partner,
            device_id_type=MESH,
        )
        copy.start()
        return copy

    first = [
        send(0, k, canvas.at[pl.ds(2 * goal[k], 2), :, 1 - near], got1.at[k], by_core)
        for k in range(steps)
    ]
    second, third, fourth = [], [], []
    for k in range(steps):
        first[k].wait_recv()
        sum1[k] = canvas[pl.ds(2 * goal[k], 2), :, near] + got1[k]
        if k % 2 == 0:
            second.append(send(1, k, sum1.at[k, :, 1 - far], got2.at[k], by_x))
        else:
            second.append(send(1, k, sum1.at[k, 1 - lo], got2.at[k], by_y))
    for k in range(steps):
        second[k].wait_recv()
        if k % 2 == 0:
            sum2[k] = sum1[k, :, far] + got2[k]
            third.append(send(2, k, sum2.at[k, 1 - lo], got3.at[k], by_y))
        else:
            sum2[k] = sum1[k, lo] + got2[k]
            third.append(send(2, k, sum2.at[k, 1 - far], got3.at[k], by_x))
    for k in range(steps):
        third[k].wait_recv()
        own = sum2[k, lo] if k % 2 == 0 else sum2[k, far]
        if k < steps - 1:
            sum3[k] = own + got3[k]
            fourth.append(send(3, k, sum3.at[k], got4.at[k], by_z[k]))
        else:
            total = own.astype(jnp.float32) + got3[k].astype(jnp.float32)
    for k in range(steps - 1):
        fourth[k].wait_recv()
        total += got4[k].astype(jnp.float32)
    out_ref[...] = total
    for copy in first + second + third + fourth:
        copy.wait_send()


def reduce_canvases(canvases, n_exp, n_grp):
    rows = PS // n_grp
    if n_grp != 4 or n_exp % 2 or n_exp > 8:
        part = lax.psum_scatter(canvases, "exp", scatter_dimension=0, tiled=True)
        part = lax.psum_scatter(part, "grp", scatter_dimension=1, tiled=True)
        return part[0].astype(jnp.float32)
    steps = n_exp // 2
    kind = canvases.dtype
    return pl.pallas_call(
        functools.partial(reduce_kernel, steps),
        out_shape=jax.ShapeDtypeStruct((rows, PS), jnp.float32),
        in_specs=[VMEM],
        out_specs=VMEM,
        scratch_shapes=[
            pltpu.VMEM((steps, 2, 2, rows, PS), kind),
            pltpu.VMEM((steps, 2, 2, rows, PS), kind),
            pltpu.VMEM((steps, 2, rows, PS), kind),
            pltpu.VMEM((steps, 2, rows, PS), kind),
            pltpu.VMEM((steps, rows, PS), kind),
            pltpu.VMEM((steps - 1, rows, PS), kind),
            pltpu.VMEM((steps - 1, rows, PS), kind),
            pltpu.SemaphoreType.DMA((4, steps)),
            pltpu.SemaphoreType.DMA((4, steps)),
        ],
        compiler_params=pltpu.CompilerParams(
            collective_id=1, has_side_effects=True, vmem_limit_bytes=40 << 20
        ),
    )(canvases.reshape(n_exp, 2, 2, rows, PS))


def per_device(
    tiles, tile_exposure, tile_patch, tile_offset, coeffs, inv_var, vert_taps, horiz_taps
):
    n_exp = lax.axis_size("exp")
    n_grp = lax.axis_size("grp")
    count, side, _ = tiles.shape
    listed = tile_patch.shape[1]
    held, terms = coeffs.shape
    f32 = jnp.float32
    top = jnp.concatenate([coeffs, inv_var[:, None]], axis=1).astype(f32)
    low = jnp.concatenate(
        [tile_exposure[:, None], tile_patch, tile_offset[:, :, 0], tile_offset[:, :, 1]], axis=1
    ).astype(f32)
    lines = -(-(held + count) // 8) * 8
    block = jnp.concatenate(
        [
            jnp.pad(top, ((0, 0), (0, 128 - top.shape[1]))),
            jnp.pad(low, ((0, lines - held - count), (0, 128 - low.shape[1]))),
        ],
        axis=0,
    )
    every = gather_blocks(block, n_exp, n_grp).reshape(n_exp * n_grp, lines, 128)
    table = every[:, :held, : terms + 1].reshape(-1, terms + 1).astype(jnp.bfloat16)
    tags = every[:, held : held + count, : low.shape[1]].reshape(-1, low.shape[1])
    names = tags[:, 0].astype(jnp.int32)
    exposures = jnp.arange(table.shape[0], dtype=jnp.int32)
    mine = jnp.dot(
        (tile_exposure[:, None] == exposures[None, :]).astype(jnp.bfloat16),
        table,
        preferred_element_type=f32,
    )
    canvases = local_canvases(
        n_exp, tile_patch, tile_offset, mine[:, :terms], mine[:, terms], tiles, vert_taps, horiz_taps
    )

    weights = jnp.dot(
        (names[:, None] == exposures[None, :]).astype(jnp.bfloat16),
        table[:, terms:],
        preferred_element_type=f32,
    )
    here = (tags[:, 1 : 1 + listed] == lax.axis_index("exp").astype(f32)).astype(f32)
    named = jnp.sum(here, axis=1, keepdims=True) > 0
    row_off = jnp.sum(here * tags[:, 1 + listed : 1 + 2 * listed], axis=1, keepdims=True)
    col_off = jnp.sum(here * tags[:, 1 + 2 * listed : 1 + 3 * listed], axis=1, keepdims=True)
    rows = PS // n_grp
    y = (jnp.arange(rows, dtype=jnp.int32) + lax.axis_index("grp") * rows).astype(f32)[None, :]
    x = jnp.arange(PS, dtype=jnp.int32).astype(f32)[None, :]
    row_mask = jnp.where(named & (y >= row_off) & (y < row_off + side), weights, 0.0)
    col_mask = (x >= col_off) & (x < col_off + side)
    cover = lax.dot_general(
        row_mask.astype(jnp.bfloat16),
        col_mask.astype(jnp.bfloat16),
        (((0,), (0,)), ((), ())),
        preferred_element_type=f32,
    )
    flux = reduce_canvases(canvases, n_exp, n_grp)
    return (flux / jnp.maximum(cover, 1.0))[None]


def solution(mesh):
    in_specs = (
        P(("exp", "grp"), None, None),
        P(("exp", "grp")),
        P(("exp", "grp"), None),
        P(("exp", "grp"), None, None),
        P(("exp", "grp"), None),
        P(("exp", "grp")),
        P(),
        P(),
    )
    out_specs = P("exp", "grp", None)
    return jax.shard_map(
        per_device, mesh=mesh, in_specs=in_specs, out_specs=out_specs, check_vma=False
    )
```

time: 305 us -> 74.1 us (0.24)
  the two profiles are of different devices: /device:TPU:0 before, /device:TPU:1 now
where the time goes in v1:
time: 74.1 us; the launch traced here: 73.7 us
  Pallas kernels  59.3 us (80%)
  local copies, waits for them, and re-layouts  8.96 us (12%)
  other arithmetic  3.24 us (4%)
  matrix products  2.12 us (3%)
    pallas_call x1, Pallas kernels, reduce_canvases(): pl.pallas_call(functools.partial(reduce_kernel, steps), out_shape=jax.Sha...  33 us
    pallas_call x1, Pallas kernels, gather_blocks(): pl.pallas_call(functools.partial(gather_kernel, n_exp, n_grp), out_shape=...  13.3 us
    pallas_call x1, Pallas kernels, local_canvases(): pl.pallas_call(functools.partial(canvas_kernel, half), grid=(patches,), o...  13 us

profile of v1, /device:TPU:1, one launch (start us, length us, event | category | flops | bytes accessed | tf_op | source)
XLA Modules:
  0.0 73.7 jit_solution(12836609236861050057)
XLA Ops:
  0.0 0.8 %copy.15 = bf16[2,1]{1,0:T(2,128)(2,1)S(1)} copy(bf16[2,1]{0,1:T(2,128)(2,1)} %bitcast.28) | data formatting | bytes 8 | tf_op jit(solution)/shard_map/broadcast_in_dim | solution.py:284
  0.8 0.7 fusion.23
  1.5 0.8 %reshape.46.patch_ref = s32[16]{0:T(128)S(1)} reshape(s32[4,4]{1,0:T(4,128)} %param.10) | data formatting | bytes 128 | tf_op jit(solution)/shard_map/reshape | solution.py:168
  2.3 0.7 %copy.16 = s32[4,1]{1,0:T(4,128)S(1)} copy(s32[4,1]{0,1:T(1,128)} %bitcast.27) | data formatting | bytes 32 | tf_op jit(solution)/shard_map/broadcast_in_dim | solution.py:302
  3.0 0.7 slice.72
  3.7 0.7 convert_element_type.55
  4.4 0.1 pad_slice_fusion.1
  4.5 0.8 %slice.73 = f32[10,4]{1,0:T(8,128)S(1)} slice(bf16[10,41]{1,0:T(8,128)(2,1)} %param.15), slice={[0:10], [37:41]} | slice | bytes 320 | tf_op jit(solution)/shard_map/jit(_roll_static)/slice | solution.py:154
  5.2 0.1 slice.64
  5.3 0.8 %rev.3 = f32[10,41]{1,0:T(8,128)S(1)} reverse(bf16[10,41]{1,0:T(8,128)(2,1)} %param.15), dimensions={1} | reverse | bytes 2460 | tf_op jit(solution)/shard_map/rev | solution.py:154
  6.1 0.1 pad_slice_fusion
  6.1 0.1 pad_maximum_fusion
  6.2 0.8 %slice_reduce_fusion.2 = (s32[4,4]{1,0:T(4,128)S(1)}, s32[4,4]{1,0:T(4,128)S(1)}, s32[4,4,1]{1,2,0:T(1,128)S(1)}, s32[4,4,1]{1,2,0:T(1,128)S(1)}) fusion(s32[4,4,2]{1,2,0:T(2,128)} %param.11), kind=kLoop, calls=%fused_computation.52 | loop fusion | bytes 384 | tf_op jit(solution)/shard_map/slice | solution.py:170
  7.0 0.8 %add_convert_fusion = f32[4,13]{1,0:T(4,128)S(1)} fusion(s32[4,4]{1,0:T(4,128)S(1)} %bitcast.26, s32[4,4]{1,0:T(4,128)S(1)} %bitcast.25, s32[4,4]{1,0:T(4,128)} %param.10, s32[4,1]{1,0:T(4,128)S(1)} %copy.16), kind=kLoop, calls=%fused_computation.35 | loop fusion | flops 208 | bytes 416 | tf_op jit(solution)/shard_map/convert_element_type | solution.py:287
  7.8 0.1 reshape_squeeze.7.col_ref
  7.8 0.1 reshape_squeeze.6.row_ref
  7.9 0.6 select_maximum_fusion.block_ref
  8.5 13.3 %shard_map.82 = f32[8,4,8,128]{3,2,1,0:T(8,128)} custom-call(f32[8,128]{1,0:T(8,128)} %select_maximum_fusion.block_ref), custom_call_target="tpu_custom_call" | custom-call | tf_op jit(solution)/shard_map/pallas_call | solution.py:64
  21.8 0.9 %slice.97 = bf16[32,2,11]{2,1,0:T(2,128)(2,1)S(1)} slice(f32[32,8,128]{2,1,0:T(8,128)} %bitcast.20), slice={[0:32], [0:2], [0:11]} | slice | bytes 2816 | tf_op jit(solution)/shard_map/slice | solution.py:297
  22.7 0.9 %slice.74 = f32[32,4,13]{2,1,0:T(4,128)S(1)} slice(f32[32,8,128]{2,1,0:T(8,128)} %bitcast.21), slice={[0:32], [2:6], [0:13]} | slice | bytes 13312 | tf_op jit(solution)/shard_map/slice | solution.py:298
  23.6 0.2 slice_reduce_fusion
  23.8 0.8 %fusion.18 = f32[4,11]{1,0:T(4,128)S(1)} fusion(bf16[64,11]{1,0:T(8,128)(2,1)S(1)} %bitcast.23, s32[4]{0:T(128)} %param.9), kind=kOutput, calls=%fused_computation.39 | convolution fusion | flops 5888 | bytes 1600 | tf_op jit(solution)/shard_map/dot_general | solution.py:301
  24.7 0.1 reshape.48.coef_ref
  24.7 0.2 slice_reduce_fusion.1.weight_ref
  24.9 0.1 fusion.9
  25.0 0.2 fusion.10
  25.3 0.2 convolution_bitcast_fusion
  25.5 0.0 copy-start
  25.5 1.0 %copy-done = bf16[4,256,256]{2,1,0:T(8,128)(2,1)S(1)} copy-done((bf16[4,256,256]{2,1,0:T(8,128)(2,1)S(1)}, bf16[4,256,256]{2,1,0:T(8,128)(2,1)}, u32[]{:S(2)}) %copy-start) | copy-done | bytes 524312
  26.6 13.0 %shard_map.83 = bf16[8,512,512]{2,1,0:T(8,128)(2,1)S(1)} custom-call(s32[16]{0:T(128)S(1)} %reshape.46.patch_ref, s32[16]{0:T(128)S(1)} %reshape_squeeze.6.row_ref, s32[16]{0:T(128)S(1)} %reshape_squeeze.7.col_ref, f32[40]{0:T(128)S(1)} %reshape.48.coef_ref, f32[4]{0:T(128)S(1)} %slice_reduce_fusion.1.weight_ref, bf16[4,256,256]{2,1,0:T(8,128)(2,1)S(1)} %copy-done, ...), custom_call_target="tpu_custom_call" | custom-call | tf_op jit(solution)/shard_map/pallas_call | solution.py:155
  39.6 33.0 %shard_map.84 = f32[128,512]{1,0:T(8,128)S(1)} custom-call(bf16[8,2,2,128,512]{4,3,2,1,0:T(8,128)(2,1)S(1)} %bitcast.17), custom_call_target="tpu_custom_call" | custom-call | tf_op jit(solution)/shard_map/pallas_call | solution.py:253
  72.6 1.1 %fusion.1 = f32[1,128,512]{2,1,0:T(8,128)} fusion(f32[128,512]{1,0:T(8,128)S(1)} %shard_map.84, f32[512]{0:T(512)S(1)} %iota_convert_fusion, f32[128]{0:T(128)S(1)} %get-tuple-element.14, f32[128]{0:T(128)S(1)} %get-tuple-element.6, bf16[128]{0:T(256)(128)(2,1)S(1)} %convolution_bitcast_fusion, f32[128]{0:T(128)S(1)} %add_convert_fusion.1, ...), kind=kOutput, calls=%fused_computation.2 | convolution fusion | flops 17186816 | bytes 529280 | tf_op jit(solution)/shard_map/dot_general | solution.py:324
  (4 shorter events, 0.0 us)
Async XLA Ops:
  25.5 1.0 %copy-start = (bf16[4,256,256]{2,1,0:T(8,128)(2,1)S(1)}, bf16[4,256,256]{2,1,0:T(8,128)(2,1)}, u32[]{:S(2)}) copy-start(bf16[4,256,256]{2,1,0:T(8,128)(2,1)} %tiles_ref.1) | copy-start | bytes 1572868

commit v2 on v1

--- a/solution.py
+++ b/solution.py
@@ -272,6 +272,253 @@
     )(canvases.reshape(n_exp, 2, 2, rows, PS))
 
 
+def fused_kernel(
+    shape, exposure_ref, patch_ref, offset_ref, top_ref, tiles_ref, taps_ref, out_ref,
+    block, held, vband, hband, weighted, canvas, got1, sum1, got2, sum2, got3, sum3, got4,
+    send_a, recv_a, send_b, recv_b, sends, recvs,
+):
+    n_exp, n_grp, own_rows, half = shape
+    steps = n_exp // 2
+    terms = vband.shape[0]
+    count, side, _ = tiles_ref.shape
+    listed = patch_ref.shape[1]
+    rows = PS // n_grp
+    lines = block.shape[0]
+    f32, i32, bf16 = jnp.float32, jnp.int32, jnp.bfloat16
+    e = lax.axis_index("exp")
+    g = lax.axis_index("grp")
+    hi, lo = e // 2, lax.rem(e, 2)
+    far, near = g // 2, lax.rem(g, 2)
+    by_core = (e, 2 * far + 1 - near)
+    by_x = (e, 2 * (1 - far) + near)
+    by_y = (2 * hi + 1 - lo, g)
+    goal = [lax.rem(hi + 1 + k, steps) for k in range(steps)]
+    by_z = [(2 * goal[k] + lo, g) for k in range(steps - 1)]
+    by_grp = [(e, lax.rem(g + i, n_grp)) for i in range(1, n_grp)]
+    by_exp = [(lax.rem(e + i, n_exp), g) for i in range(1, n_exp)]
+
+    barrier = pltpu.get_barrier_semaphore()
+    for partner in by_grp + by_exp:
+        pl.semaphore_signal(barrier, inc=1, device_id=partner, device_id_type=MESH)
+
+    line = lax.broadcasted_iota(i32, (lines, 128), 0)
+    lane = lax.broadcasted_iota(i32, (lines, 128), 1)
+    data = top_ref[...]
+    for t in range(count):
+        values = [exposure_ref[t]] + [patch_ref[t, j] for j in range(listed)]
+        values += [offset_ref[t, 2 * j + c] for c in range(2) for j in range(listed)]
+        for n, value in enumerate(values):
+            data = jnp.where((line == own_rows + t) & (lane == n), value.astype(f32), data)
+    block[...] = data
+    held[e, g] = data
+
+    pl.semaphore_wait(barrier, n_grp + n_exp - 2)
+
+    def copy_to(src, dst, send_sem, recv_sem, partner):
+        copy = pltpu.make_async_remote_copy(
+            src_ref=src, dst_ref=dst, send_sem=send_sem, recv_sem=recv_sem,
+            device_id=partner, device_id_type=MESH,
+        )
+        copy.start()
+        return copy
+
+    row = lax.broadcasted_iota(i32, (side, side), 0)
+    col = lax.broadcasted_iota(i32, (side, side), 1)
+    inside = jnp.abs(col - row) <= half
+
+    def build(band, base):
+        def one(b, carry):
+            taps = jnp.broadcast_to(taps_ref[pl.ds(base + b, 1), :], (side, side))
+            taps = pltpu.roll(taps, side - half // 8 * 8, 1, stride=1, stride_axis=0)
+            band[b] = jnp.where(inside, taps, 0.0).astype(bf16)
+            return carry
+
+        lax.fori_loop(0, terms, one, 0)
+
+    copies = [
+        copy_to(block, held.at[e, g], send_a.at[i], recv_a.at[i], partner)
+        for i, partner in enumerate(by_grp)
+    ]
+    build(hband, terms)
+    for copy in copies:
+        copy.wait()
+    copies = [
+        copy_to(held.at[e], held.at[e], send_b.at[i], recv_b.at[i], partner)
+        for i, partner in enumerate(by_exp)
+    ]
+    build(vband, 0)
+    for copy in copies:
+        copy.wait()
+
+    every = held[...].reshape(n_exp * n_grp * lines, 128)
+    total_lines = n_exp * n_grp * lines
+    spot = lax.broadcasted_iota(i32, (total_lines, 128), 0)
+    number = jnp.where(spot % lines < own_rows, spot // lines * own_rows + spot % lines, -1)
+
+    def convolve(t, carry):
+        mine = jnp.sum(jnp.where(number == exposure_ref[t], every, 0.0), axis=0, keepdims=True)
+        tile = tiles_ref[t]
+        total = jnp.zeros((side, side), f32)
+        for b in range(terms):
+            across = jnp.dot(tile, hband[b], preferred_element_type=f32)
+            part = (across * mine[:, b : b + 1]).astype(bf16)
+            total += jnp.dot(vband[b], part, preferred_element_type=f32)
+        weighted[t] = (mine[:, terms : terms + 1] * total).astype(bf16)
+        return carry
+
+    lax.fori_loop(0, count, convolve, 0)
+
+    inner_c = lax.broadcasted_iota(i32, (side, PS), 1) - lax.broadcasted_iota(i32, (side, PS), 0)
+    inner_r = lax.broadcasted_iota(i32, (PS, side), 0) - lax.broadcasted_iota(i32, (PS, side), 1)
+
+    def place(k):
+        def one(y, carry):
+            patch = 2 * goal[k] + y
+            picked = [[i32(0), i32(-4 * PS), i32(-4 * PS)] for _ in range(2)]
+            found = i32(0)
+            for t in range(count):
+                for j in range(listed):
+                    hit = patch_ref[t, j] == patch
+                    new = (i32(t), offset_ref[t, 2 * j], offset_ref[t, 2 * j + 1])
+                    for slot in range(2):
+                        take = hit & (found == slot)
+                        picked[slot] = [
+                            jnp.where(take, a, b) for a, b in zip(new, picked[slot])
+                        ]
+                    found = found + jnp.where(hit, 1, 0)
+            image = jnp.zeros((PS, PS), f32)
+            for t, row_off, col_off in picked:
+                col_pick = jnp.where(inner_c == col_off, 1.0, 0.0).astype(bf16)
+                row_pick = jnp.where(inner_r == row_off, 1.0, 0.0).astype(bf16)
+                moved = jnp.dot(weighted[t], col_pick, preferred_element_type=f32)
+                image += jnp.dot(row_pick, moved.astype(bf16), preferred_element_type=f32)
+            canvas[k, y] = image.astype(bf16).reshape(2, 2, rows, PS)
+            return carry
+
+        lax.fori_loop(0, 2, one, 0)
+
+    def send(stage, k, src, dst, partner):
+        return copy_to(src, dst, sends.at[stage, k], recvs.at[stage, k], partner)
+
+    first, second, third, fourth = [], [], [], []
+
+    def second_step(k):
+        first[k].wait_recv()
+        sum1[k] = canvas[k, :, :, near] + got1[k]
+        if k % 2 == 0:
+            second.append(send(1, k, sum1.at[k, :, 1 - far], got2.at[k], by_x))
+        else:
+            second.append(send(1, k, sum1.at[k, 1 - lo], got2.at[k], by_y))
+
+    for k in range(steps):
+        place(k)
+        first.append(send(0, k, canvas.at[k, :, :, 1 - near], got1.at[k], by_core))
+        if k > 0:
+            second_step(k - 1)
+    second_step(steps - 1)
+
+    tag = lambda n: every[:, n : n + 1]
+    row_off = jnp.full((total_lines, 1), -4.0 * PS, f32)
+    col_off = row_off
+    for j in range(listed):
+        hit = tag(1 + j) == e.astype(f32)
+        row_off = jnp.where(hit, tag(1 + listed + j), row_off)
+        col_off = jnp.where(hit, tag(1 + 2 * listed + j), col_off)
+    down = lax.broadcasted_iota(i32, (total_lines, total_lines), 1)
+    down = jnp.where(down % lines < own_rows, down // lines * own_rows + down % lines, -1)
+    chosen = jnp.where(tag(0) == down.astype(f32), 1.0, 0.0).astype(bf16)
+    weights = jnp.dot(chosen, every.astype(bf16), preferred_element_type=f32)
+    weights = weights[:, terms : terms + 1]
+    kept = lax.broadcasted_iota(i32, (total_lines, 1), 0) % lines
+    weights = jnp.where((kept >= own_rows) & (kept < own_rows + count), weights, 0.0)
+    y = (lax.broadcasted_iota(i32, (total_lines, rows), 1) + g * rows).astype(f32)
+    x = lax.broadcasted_iota(i32, (total_lines, PS), 1).astype(f32)
+    row_mask = jnp.where((y >= row_off) & (y < row_off + side), weights, 0.0).astype(bf16)
+    col_mask = jnp.where((x >= col_off) & (x < col_off + side), 1.0, 0.0).astype(bf16)
+    cover = lax.dot_general(
+        row_mask, col_mask, (((0,), (0,)), ((), ())), preferred_element_type=f32
+    )
+    out_ref[0] = jnp.maximum(cover, 1.0)
+
+    for k in range(steps):
+        second[k].wait_recv()
+        if k % 2 == 0:
+            sum2[k] = sum1[k, :, far] + got2[k]
+            third.append(send(2, k, sum2.at[k, 1 - lo], got3.at[k], by_y))
+        else:
+            sum2[k] = sum1[k, lo] + got2[k]
+            third.append(send(2, k, sum2.at[k, 1 - far], got3.at[k], by_x))
+    for k in range(steps):
+        third[k].wait_recv()
+        own = sum2[k, lo] if k % 2 == 0 else sum2[k, far]
+        if k < steps - 1:
+            sum3[k] = own + got3[k]
+            fourth.append(send(3, k, sum3.at[k], got4.at[k], by_z[k]))
+        else:
+            total = own.astype(f32) + got3[k].astype(f32)
+    for k in range(steps - 1):
+        fourth[k].wait_recv()
+        total += got4[k].astype(f32)
+    out_ref[0] = total / out_ref[0]
+    for copy in first + second + third + fourth:
+        copy.wait_send()
+
+
+def fused(
+    n_exp, n_grp, tiles, tile_exposure, tile_patch, tile_offset, coeffs, inv_var, vtaps, htaps
+):
+    count, side, _ = tiles.shape
+    terms, width = vtaps.shape
+    half = (width - 1) // 2
+    own_rows = coeffs.shape[0]
+    lines = -(-(own_rows + count) // 8) * 8
+    rows = PS // n_grp
+    steps = n_exp // 2
+    f32, kind = jnp.float32, jnp.bfloat16
+    top = jnp.concatenate([coeffs, inv_var[:, None]], axis=1).astype(f32)
+    top = jnp.pad(top, ((0, lines - own_rows), (0, 128 - terms - 1)))
+    taps = jnp.concatenate([vtaps, htaps[:, ::-1]], axis=0).astype(f32)
+    taps = jnp.concatenate(
+        [
+            taps[:, half % 8 :],
+            jnp.zeros((2 * terms, side - width), f32),
+            taps[:, : half % 8],
+        ],
+        axis=1,
+    )
+    dma = pltpu.SemaphoreType.DMA
+    return pl.pallas_call(
+        functools.partial(fused_kernel, (n_exp, n_grp, own_rows, half)),
+        out_shape=jax.ShapeDtypeStruct((1, rows, PS), f32),
+        in_specs=[SMEM] * 3 + [VMEM] * 3,
+        out_specs=VMEM,
+        scratch_shapes=[
+            pltpu.VMEM((lines, 128), f32),
+            pltpu.VMEM((n_exp, n_grp, lines, 128), f32),
+            pltpu.VMEM((terms, side, side), kind),
+            pltpu.VMEM((terms, side, side), kind),
+            pltpu.VMEM((count, side, side), kind),
+            pltpu.VMEM((steps, 2, 2, 2, rows, PS), kind),
+            pltpu.VMEM((steps, 2, 2, rows, PS), kind),
+            pltpu.VMEM((steps, 2, 2, rows, PS), kind),
+            pltpu.VMEM((steps, 2, rows, PS), kind),
+            pltpu.VMEM((steps, 2, rows, PS), kind),
+            pltpu.VMEM((steps, rows, PS), kind),
+            pltpu.VMEM((steps - 1, rows, PS), kind),
+            pltpu.VMEM((steps - 1, rows, PS), kind),
+            dma((n_grp - 1,)),
+            dma((n_grp - 1,)),
+            dma((n_exp - 1,)),
+            dma((n_exp - 1,)),
+            dma((4, steps)),
+            dma((4, steps)),
+        ],
+        compiler_params=pltpu.CompilerParams(
+            collective_id=2, has_side_effects=True, vmem_limit_bytes=48 << 20
+        ),
+    )(tile_exposure, tile_patch, tile_offset.reshape(count, -1), top, tiles, taps)
+
+
 def per_device(
     tiles, tile_exposure, tile_patch, tile_offset, coeffs, inv_var, vert_taps, horiz_taps
 ):
@@ -281,6 +528,11 @@
     listed = tile_patch.shape[1]
     held, terms = coeffs.shape
     f32 = jnp.float32
+    if n_grp == 4 and n_exp % 2 == 0 and 4 <= n_exp <= 8:
+        return fused(
+            n_exp, n_grp, tiles, tile_exposure, tile_patch, tile_offset, coeffs, inv_var,
+            vert_taps, horiz_taps,
+        )
     top = jnp.concatenate([coeffs, inv_var[:, None]], axis=1).astype(f32)
     low = jnp.concatenate(
         [tile_exposure[:, None], tile_patch, tile_offset[:, :, 0], tile_offset[:, :, 1]], axis=1

time: 74.1 us -> 58.1 us (0.78)
  the two profiles are of different devices: /device:TPU:1 before, /device:TPU:0 now
where the time goes in v2:
time: 58.1 us; the launch traced here: 57.8 us
  Pallas kernels  52.3 us (90%)
  local copies, waits for them, and re-layouts  5.32 us (9%)
    pallas_call x1, Pallas kernels, fused(): pl.pallas_call(functools.partial(fused_kernel, (n_exp, n_grp, own_rows, h...  52.3 us
    unnamed x18, local copies, waits for them, and re-layouts  4.89 us

profile of v2, /device:TPU:0, one launch (start us, length us, event | category | flops | bytes accessed | tf_op | source)
XLA Modules:
  0.0 57.8 jit_solution(11787959041371151309)
XLA Ops:
  0.0 0.0 copy-start.7
  0.0 0.7 %copy-done.7 = bf16[2]{0:T(256)(128)(2,1)S(1)} copy-done((bf16[2]{0:T(256)(128)(2,1)S(1)}, bf16[2]{0:T(256)(128)(2,1)}, u32[]{:S(2)}) %copy-start.7) | copy-done | bytes 28
  0.7 0.1 copy.10
  0.8 0.0 copy-start.6
  0.8 0.0 copy-start.4
  0.8 0.1 pad.9.clone
  0.8 0.6 copy-done.6
  1.4 0.1 fusion.6.top_ref
  1.5 0.0 copy-done.4
  1.5 0.1 copy.9
  1.6 0.0 copy-start.5
  1.6 0.1 copy.11.offset_ref
  1.7 0.6 %copy-done.5 = bf16[10,41]{1,0:T(8,128)(2,1)S(1)} copy-done((bf16[10,41]{1,0:T(8,128)(2,1)S(1)}, bf16[10,41]{1,0:T(8,128)(2,1)}, u32[]{:S(2)}) %copy-start.5) | copy-done | bytes 844
  2.3 0.0 copy-start.3
  2.3 0.1 rev.3
  2.4 0.6 %copy-done.3 = bf16[10,41]{1,0:T(8,128)(2,1)S(1)} copy-done((bf16[10,41]{1,0:T(8,128)(2,1)S(1)}, bf16[10,41]{1,0:T(8,128)(2,1)}, u32[]{:S(2)}) %copy-start.3) | copy-done | bytes 844
  3.0 0.1 slice.8
  3.1 0.0 copy-start.1
  3.1 0.0 copy-start.2
  3.1 0.1 pad_maximum_fusion.taps_ref
  3.1 0.6 %copy-done.1 = s32[4,4]{1,0:T(4,128)S(1)} copy-done((s32[4,4]{1,0:T(4,128)S(1)}, s32[4,4]{1,0:T(4,128)}, u32[]{:S(2)}) %copy-start.1) | copy-done | bytes 88
  3.7 0.0 copy-done.2
  3.7 0.0 copy-start
  3.7 1.0 %copy-done = bf16[4,256,256]{2,1,0:T(8,128)(2,1)S(1)} copy-done((bf16[4,256,256]{2,1,0:T(8,128)(2,1)S(1)}, bf16[4,256,256]{2,1,0:T(8,128)(2,1)}, u32[]{:S(2)}) %copy-start) | copy-done | bytes 524312
  4.8 52.3 %shard_map.82 = f32[1,128,512]{2,1,0:T(8,128)S(1)} custom-call(s32[4]{0:T(128)S(1)} %copy-done.2, s32[4,4]{1,0:T(4,128)S(1)} %copy-done.1, s32[4,8]{1,0:T(4,128)S(1)} %copy.11.offset_ref, f32[8,128]{1,0:T(8,128)S(1)} %fusion.6.top_ref, bf16[4,256,256]{2,1,0:T(8,128)(2,1)S(1)} %copy-done, f32[20,256]{1,0:T(8,128)S(1)} %pad_maximum_fusion.taps_ref), custom_call_target="tpu_custom_call" | custom-call | tf_op jit(solution)/shard_map/pallas_call | solution.py:490
  57.1 0.7 %copy.13 = f32[1,128,512]{2,1,0:T(8,128)} copy(f32[1,128,512]{2,1,0:T(8,128)S(1)} %shard_map.82) | data formatting | bytes 524288
  (2 shorter events, 0.0 us)
Async XLA Ops:
  0.0 0.7 %copy-start.7 = (bf16[2]{0:T(256)(128)(2,1)S(1)}, bf16[2]{0:T(256)(128)(2,1)}, u32[]{:S(2)}) copy-start(bf16[2]{0:T(256)(128)(2,1)} %param.13) | copy-start | bytes 16
  0.8 0.7 %copy-start.6 = (bf16[2,10]{1,0:T(2,128)(2,1)S(1)}, bf16[2,10]{1,0:T(2,128)(2,1)}, u32[]{:S(2)}) copy-start(bf16[2,10]{1,0:T(2,128)(2,1)} %param.12) | copy-start | bytes 124
  0.8 0.7 %copy-start.4 = (s32[4,4,2]{1,2,0:T(2,128)S(1)}, s32[4,4,2]{1,2,0:T(2,128)}, u32[]{:S(2)}) copy-start(s32[4,4,2]{1,2,0:T(2,128)} %param.11) | copy-start | bytes 388
  1.6 0.7 %copy-start.5 = (bf16[10,41]{1,0:T(8,128)(2,1)S(1)}, bf16[10,41]{1,0:T(8,128)(2,1)}, u32[]{:S(2)}) copy-start(bf16[10,41]{1,0:T(8,128)(2,1)} %param.15) | copy-start | bytes 2464
  2.3 0.7 %copy-start.3 = (bf16[10,41]{1,0:T(8,128)(2,1)S(1)}, bf16[10,41]{1,0:T(8,128)(2,1)}, u32[]{:S(2)}) copy-start(bf16[10,41]{1,0:T(8,128)(2,1)} %param.14) | copy-start | bytes 2464
  3.1 0.7 %copy-start.1 = (s32[4,4]{1,0:T(4,128)S(1)}, s32[4,4]{1,0:T(4,128)}, u32[]{:S(2)}) copy-start(s32[4,4]{1,0:T(4,128)} %patch_ref.1) | copy-start | bytes 196
  3.1 0.7 %copy-start.2 = (s32[4]{0:T(128)S(1)}, s32[4]{0:T(128)}, u32[]{:S(2)}) copy-start(s32[4]{0:T(128)} %exposure_ref.1) | copy-start | bytes 52
  3.7 1.0 %copy-start = (bf16[4,256,256]{2,1,0:T(8,128)(2,1)S(1)}, bf16[4,256,256]{2,1,0:T(8,128)(2,1)}, u32[]{:S(2)}) copy-start(bf16[4,256,256]{2,1,0:T(8,128)(2,1)} %tiles_ref.1) | copy-start | bytes 1572868

commit v3 on v2

--- a/solution.py
+++ b/solution.py
@@ -292,7 +292,8 @@
     by_core = (e, 2 * far + 1 - near)
     by_x = (e, 2 * (1 - far) + near)
     by_y = (2 * hi + 1 - lo, g)
-    goal = [lax.rem(hi + 1 + k, steps) for k in range(steps)]
+    hops = (2, 1, 3, 0) if steps == 4 else (1, 0)
+    goal = [lax.rem(hi + hop, steps) for hop in hops]
     by_z = [(2 * goal[k] + lo, g) for k in range(steps - 1)]
     by_grp = [(e, lax.rem(g + i, n_grp)) for i in range(1, n_grp)]
     by_exp = [(lax.rem(e + i, n_exp), g) for i in range(1, n_exp)]
@@ -400,22 +401,53 @@
     def send(stage, k, src, dst, partner):
         return copy_to(src, dst, sends.at[stage, k], recvs.at[stage, k], partner)
 
-    first, second, third, fourth = [], [], [], []
+    first, second, rest, third, fourth = [], [], [], [], []
+
+    def first_step(k):
+        place(k)
+        first.append(send(0, k, canvas.at[k, :, :, 1 - near], got1.at[k], by_core))
 
     def second_step(k):
         first[k].wait_recv()
         sum1[k] = canvas[k, :, :, near] + got1[k]
+        give = sum1.at[k, 1 - lo, 1 - far]
         if k % 2 == 0:
-            second.append(send(1, k, sum1.at[k, :, 1 - far], got2.at[k], by_x))
+            second.append(send(1, k, give, got2.at[k, 1 - lo], by_x))
+            rest.append(send(4, k, sum1.at[k, lo, 1 - far], got2.at[k, lo], by_x))
         else:
-            second.append(send(1, k, sum1.at[k, 1 - lo], got2.at[k], by_y))
-
-    for k in range(steps):
-        place(k)
-        first.append(send(0, k, canvas.at[k, :, :, 1 - near], got1.at[k], by_core))
-        if k > 0:
-            second_step(k - 1)
-    second_step(steps - 1)
+            second.append(send(1, k, give, got2.at[k, 1 - far], by_y))
+            rest.append(send(4, k, sum1.at[k, 1 - lo, far], got2.at[k, far], by_y))
+
+    def third_step(k):
+        second[k].wait_recv()
+        if k % 2 == 0:
+            sum2[k] = sum1[k, 1 - lo, far] + got2[k, 1 - lo]
+        else:
+            sum2[k] = sum1[k, lo, 1 - far] + got2[k, 1 - far]
+        third.append(send(2, k, sum2.at[k], got3.at[k], by_y if k % 2 == 0 else by_x))
+
+    def owned(k):
+        rest[k].wait_recv()
+        third[k].wait_recv()
+        across = got2[k, lo] if k % 2 == 0 else got2[k, far]
+        return sum1[k, lo, far].astype(f32) + across.astype(f32) + got3[k].astype(f32)
+
+    def fourth_step(k):
+        sum3[k] = owned(k).astype(bf16)
+        fourth.append(send(3, k, sum3.at[k], got4.at[k], by_z[k]))
+
+    first_step(0)
+    first_step(1)
+    second_step(0)
+    second_step(1)
+    if steps > 2:
+        first_step(2)
+    third_step(0)
+    third_step(1)
+    if steps > 2:
+        first_step(3)
+        second_step(2)
+        second_step(3)
 
     tag = lambda n: every[:, n : n + 1]
     row_off = jnp.full((total_lines, 1), -4.0 * PS, f32)
@@ -440,27 +472,18 @@
     )
     out_ref[0] = jnp.maximum(cover, 1.0)
 
-    for k in range(steps):
-        second[k].wait_recv()
-        if k % 2 == 0:
-            sum2[k] = sum1[k, :, far] + got2[k]
-            third.append(send(2, k, sum2.at[k, 1 - lo], got3.at[k], by_y))
-        else:
-            sum2[k] = sum1[k, lo] + got2[k]
-            third.append(send(2, k, sum2.at[k, 1 - far], got3.at[k], by_x))
-    for k in range(steps):
-        third[k].wait_recv()
-        own = sum2[k, lo] if k % 2 == 0 else sum2[k, far]
-        if k < steps - 1:
-            sum3[k] = own + got3[k]
-            fourth.append(send(3, k, sum3.at[k], got4.at[k], by_z[k]))
-        else:
-            total = own.astype(f32) + got3[k].astype(f32)
+    fourth_step(0)
+    if steps > 2:
+        fourth_step(1)
+        third_step(2)
+        third_step(3)
+        fourth_step(2)
+    total = owned(steps - 1)
     for k in range(steps - 1):
         fourth[k].wait_recv()
         total += got4[k].astype(f32)
     out_ref[0] = total / out_ref[0]
-    for copy in first + second + third + fourth:
+    for copy in first + second + rest + third + fourth:
         copy.wait_send()
 
 
@@ -502,7 +525,7 @@
             pltpu.VMEM((steps, 2, 2, rows, PS), kind),
             pltpu.VMEM((steps, 2, 2, rows, PS), kind),
             pltpu.VMEM((steps, 2, rows, PS), kind),
-            pltpu.VMEM((steps, 2, rows, PS), kind),
+            pltpu.VMEM((steps, rows, PS), kind),
             pltpu.VMEM((steps, rows, PS), kind),
             pltpu.VMEM((steps - 1, rows, PS), kind),
             pltpu.VMEM((steps - 1, rows, PS), kind),
@@ -510,8 +533,8 @@
             dma((n_grp - 1,)),
             dma((n_exp - 1,)),
             dma((n_exp - 1,)),
-            dma((4, steps)),
-            dma((4, steps)),
+            dma((5, steps)),
+            dma((5, steps)),
         ],
         compiler_params=pltpu.CompilerParams(
             collective_id=2, has_side_effects=True, vmem_limit_bytes=48 << 20
@@ -528,7 +551,7 @@
     listed = tile_patch.shape[1]
     held, terms = coeffs.shape
     f32 = jnp.float32
-    if n_grp == 4 and n_exp % 2 == 0 and 4 <= n_exp <= 8:
+    if n_grp == 4 and n_exp in (4, 8):
         return fused(
             n_exp, n_grp, tiles, tile_exposure, tile_patch, tile_offset, coeffs, inv_var,
             vert_taps, horiz_taps,

time: 58.1 us -> 53.6 us (0.923)
  Pallas kernels: 52.3 us -> 47.8 us
    pallas_call x1, Pallas kernels: 52.3 us -> 47.8 us  [fused(): pl.pallas_call(functools.partial(fused_kernel, (n_exp, n_grp, own_rows, h...]
where the time goes in v3:
time: 53.6 us; the launch traced here: 53.3 us
  Pallas kernels  47.8 us (89%)
  local copies, waits for them, and re-layouts  5.32 us (10%)
    pallas_call x1, Pallas kernels, fused(): pl.pallas_call(functools.partial(fused_kernel, (n_exp, n_grp, own_rows, h...  47.8 us
    unnamed x18, local copies, waits for them, and re-layouts  4.89 us

profile of v3, /device:TPU:0, one launch (start us, length us, event | category | flops | bytes accessed | tf_op | source)
XLA Modules:
  0.0 53.3 jit_solution(462879553630788860)
XLA Ops:
  0.0 0.0 copy-start.7
  0.0 0.7 %copy-done.7 = bf16[2]{0:T(256)(128)(2,1)S(1)} copy-done((bf16[2]{0:T(256)(128)(2,1)S(1)}, bf16[2]{0:T(256)(128)(2,1)}, u32[]{:S(2)}) %copy-start.7) | copy-done | bytes 28
  0.7 0.1 copy.10
  0.8 0.0 copy-start.6
  0.8 0.0 copy-start.4
  0.8 0.1 pad.9.clone
  0.8 0.6 %copy-done.6 = bf16[2,10]{1,0:T(2,128)(2,1)S(1)} copy-done((bf16[2,10]{1,0:T(2,128)(2,1)S(1)}, bf16[2,10]{1,0:T(2,128)(2,1)}, u32[]{:S(2)}) %copy-start.6) | copy-done | bytes 64
  1.4 0.1 fusion.6.top_ref
  1.5 0.0 copy-done.4
  1.5 0.1 copy.9
  1.6 0.0 copy-start.5
  1.6 0.1 copy.11.offset_ref
  1.7 0.6 %copy-done.5 = bf16[10,41]{1,0:T(8,128)(2,1)S(1)} copy-done((bf16[10,41]{1,0:T(8,128)(2,1)S(1)}, bf16[10,41]{1,0:T(8,128)(2,1)}, u32[]{:S(2)}) %copy-start.5) | copy-done | bytes 844
  2.3 0.0 copy-start.3
  2.3 0.1 rev.3
  2.4 0.6 %copy-done.3 = bf16[10,41]{1,0:T(8,128)(2,1)S(1)} copy-done((bf16[10,41]{1,0:T(8,128)(2,1)S(1)}, bf16[10,41]{1,0:T(8,128)(2,1)}, u32[]{:S(2)}) %copy-start.3) | copy-done | bytes 844
  3.0 0.1 slice.8
  3.1 0.0 copy-start.1
  3.1 0.0 copy-start.2
  3.1 0.1 pad_maximum_fusion.taps_ref
  3.1 0.6 %copy-done.1 = s32[4,4]{1,0:T(4,128)S(1)} copy-done((s32[4,4]{1,0:T(4,128)S(1)}, s32[4,4]{1,0:T(4,128)}, u32[]{:S(2)}) %copy-start.1) | copy-done | bytes 88
  3.7 0.0 copy-done.2
  3.7 0.0 copy-start
  3.7 1.0 %copy-done = bf16[4,256,256]{2,1,0:T(8,128)(2,1)S(1)} copy-done((bf16[4,256,256]{2,1,0:T(8,128)(2,1)S(1)}, bf16[4,256,256]{2,1,0:T(8,128)(2,1)}, u32[]{:S(2)}) %copy-start) | copy-done | bytes 524312
  4.8 47.8 %shard_map.82 = f32[1,128,512]{2,1,0:T(8,128)S(1)} custom-call(s32[4]{0:T(128)S(1)} %copy-done.2, s32[4,4]{1,0:T(4,128)S(1)} %copy-done.1, s32[4,8]{1,0:T(4,128)S(1)} %copy.11.offset_ref, f32[8,128]{1,0:T(8,128)S(1)} %fusion.6.top_ref, bf16[4,256,256]{2,1,0:T(8,128)(2,1)S(1)} %copy-done, f32[20,256]{1,0:T(8,128)S(1)} %pad_maximum_fusion.taps_ref), custom_call_target="tpu_custom_call" | custom-call | tf_op jit(solution)/shard_map/pallas_call | solution.py:513
  52.6 0.7 %copy.13 = f32[1,128,512]{2,1,0:T(8,128)} copy(f32[1,128,512]{2,1,0:T(8,128)S(1)} %shard_map.82) | data formatting | bytes 524288
  (2 shorter events, 0.0 us)
Async XLA Ops:
  0.0 0.7 %copy-start.7 = (bf16[2]{0:T(256)(128)(2,1)S(1)}, bf16[2]{0:T(256)(128)(2,1)}, u32[]{:S(2)}) copy-start(bf16[2]{0:T(256)(128)(2,1)} %param.13) | copy-start | bytes 16
  0.8 0.7 %copy-start.6 = (bf16[2,10]{1,0:T(2,128)(2,1)S(1)}, bf16[2,10]{1,0:T(2,128)(2,1)}, u32[]{:S(2)}) copy-start(bf16[2,10]{1,0:T(2,128)(2,1)} %param.12) | copy-start | bytes 124
  0.8 0.7 %copy-start.4 = (s32[4,4,2]{1,2,0:T(2,128)S(1)}, s32[4,4,2]{1,2,0:T(2,128)}, u32[]{:S(2)}) copy-start(s32[4,4,2]{1,2,0:T(2,128)} %param.11) | copy-start | bytes 388
  1.6 0.7 %copy-start.5 = (bf16[10,41]{1,0:T(8,128)(2,1)S(1)}, bf16[10,41]{1,0:T(8,128)(2,1)}, u32[]{:S(2)}) copy-start(bf16[10,41]{1,0:T(8,128)(2,1)} %param.15) | copy-start | bytes 2464
  2.3 0.7 %copy-start.3 = (bf16[10,41]{1,0:T(8,128)(2,1)S(1)}, bf16[10,41]{1,0:T(8,128)(2,1)}, u32[]{:S(2)}) copy-start(bf16[10,41]{1,0:T(8,128)(2,1)} %param.14) | copy-start | bytes 2464
  3.1 0.7 %copy-start.1 = (s32[4,4]{1,0:T(4,128)S(1)}, s32[4,4]{1,0:T(4,128)}, u32[]{:S(2)}) copy-start(s32[4,4]{1,0:T(4,128)} %patch_ref.1) | copy-start | bytes 196
  3.1 0.7 %copy-start.2 = (s32[4]{0:T(128)S(1)}, s32[4]{0:T(128)}, u32[]{:S(2)}) copy-start(s32[4]{0:T(128)} %exposure_ref.1) | copy-start | bytes 52
  3.7 1.0 %copy-start = (bf16[4,256,256]{2,1,0:T(8,128)(2,1)S(1)}, bf16[4,256,256]{2,1,0:T(8,128)(2,1)}, u32[]{:S(2)}) copy-start(bf16[4,256,256]{2,1,0:T(8,128)(2,1)} %tiles_ref.1) | copy-start | bytes 1572868

commit v4 on v3

--- a/solution.py
+++ b/solution.py
@@ -273,9 +273,9 @@
 
 
 def fused_kernel(
-    shape, exposure_ref, patch_ref, offset_ref, top_ref, tiles_ref, taps_ref, out_ref,
+    shape, exposure_ref, patch_ref, offset_ref, top_ref, tiles_hbm, taps_ref, out_ref,
     block, held, vband, hband, weighted, canvas, got1, sum1, got2, sum2, got3, sum3, got4,
-    send_a, recv_a, send_b, recv_b, sends, recvs,
+    send_a, recv_a, send_b, recv_b, sends, recvs, tiles_ref, tiles_sem,
 ):
     n_exp, n_grp, own_rows, half = shape
     steps = n_exp // 2
@@ -298,6 +298,8 @@
     by_grp = [(e, lax.rem(g + i, n_grp)) for i in range(1, n_grp)]
     by_exp = [(lax.rem(e + i, n_exp), g) for i in range(1, n_exp)]
 
+    fetch = pltpu.make_async_copy(tiles_hbm, tiles_ref, tiles_sem)
+    fetch.start()
     barrier = pltpu.get_barrier_semaphore()
     for partner in by_grp + by_exp:
         pl.semaphore_signal(barrier, inc=1, device_id=partner, device_id_type=MESH)
@@ -367,6 +369,7 @@
         weighted[t] = (mine[:, terms : terms + 1] * total).astype(bf16)
         return carry
 
+    fetch.wait()
     lax.fori_loop(0, count, convolve, 0)
 
     inner_c = lax.broadcasted_iota(i32, (side, PS), 1) - lax.broadcasted_iota(i32, (side, PS), 0)
@@ -513,7 +516,7 @@
     return pl.pallas_call(
         functools.partial(fused_kernel, (n_exp, n_grp, own_rows, half)),
         out_shape=jax.ShapeDtypeStruct((1, rows, PS), f32),
-        in_specs=[SMEM] * 3 + [VMEM] * 3,
+        in_specs=[SMEM] * 3 + [VMEM, pl.BlockSpec(memory_space=pltpu.HBM), VMEM],
         out_specs=VMEM,
         scratch_shapes=[
             pltpu.VMEM((lines, 128), f32),
@@ -535,9 +538,11 @@
             dma((n_exp - 1,)),
             dma((5, steps)),
             dma((5, steps)),
+            pltpu.VMEM(tiles.shape, tiles.dtype),
+            dma,
         ],
         compiler_params=pltpu.CompilerParams(
-            collective_id=2, has_side_effects=True, vmem_limit_bytes=48 << 20
+            collective_id=2, has_side_effects=True, vmem_limit_bytes=(64 << 20) - (256 << 10)
         ),
     )(tile_exposure, tile_patch, tile_offset.reshape(count, -1), top, tiles, taps)
 

time: 53.6 us -> 55 us (1.026)
  other arithmetic: 0.16 us -> 1.36 us
  Pallas kernels: 47.8 us -> 48.6 us
  local copies, waits for them, and re-layouts: 5.32 us -> 4.63 us
    unnamed x18 -> x12, local copies, waits for them, and re-layouts: 4.89 us -> 3.65 us
    pallas_call x1, Pallas kernels: 47.8 us -> 48.6 us  [fused(): pl.pallas_call(functools.partial(fused_kernel, (n_exp, n_grp, own_rows, h...]
    concatenate x1, other arithmetic: 0.08 us -> 0.69 us  [fused(): jnp.concatenate([taps[:, half % 8:], jnp.zeros((2 * terms, side - width),...]
    pad x1, other arithmetic: 0.08 us -> 0.66 us  [fused(): top = jnp.pad(top, ((0, lines - own_rows), (0, 128 - terms - 1)))]
    reshape x1, local copies, waits for them, and re-layouts: 0.08 us -> 0.64 us  [fused(): tile_offset.reshape(count, -1)]
where the time goes in v4:
time: 55 us; the launch traced here: 54.7 us
  Pallas kernels  48.6 us (88%)
  local copies, waits for them, and re-layouts  4.63 us (8%)
  other arithmetic  1.36 us (2%)
    pallas_call x1, Pallas kernels, fused(): pl.pallas_call(functools.partial(fused_kernel, (n_exp, n_grp, own_rows, h...  48.6 us
    unnamed x12, local copies, waits for them, and re-layouts  3.65 us

profile of v4, /device:TPU:0, one launch (start us, length us, event | category | flops | bytes accessed | tf_op | source)
XLA Modules:
  0.0 54.7 jit_solution(909892426713223906)
XLA Ops:
  0.0 0.0 copy-start.4
  0.0 0.7 %copy-done.4 = bf16[2]{0:T(256)(128)(2,1)S(1)} copy-done((bf16[2]{0:T(256)(128)(2,1)S(1)}, bf16[2]{0:T(256)(128)(2,1)}, u32[]{:S(2)}) %copy-start.4) | copy-done | bytes 28
  0.7 0.1 copy.10
  0.8 0.0 copy-start.3
  0.8 0.0 copy-start.1
  0.8 0.1 pad.9.clone
  0.8 0.6 %copy-done.3 = bf16[2,10]{1,0:T(2,128)(2,1)S(1)} copy-done((bf16[2,10]{1,0:T(2,128)(2,1)S(1)}, bf16[2,10]{1,0:T(2,128)(2,1)}, u32[]{:S(2)}) %copy-start.3) | copy-done | bytes 64
  1.4 0.7 %fusion.6.top_ref = f32[8,128]{1,0:T(8,128)} fusion(bf16[2,1]{1,0:T(2,128)(2,1)S(1)} %copy.10, bf16[2,10]{1,0:T(2,128)(2,1)S(1)} %copy-done.3), kind=kLoop, calls=%fused_computation.10 | loop fusion | flops 11264 | bytes 4140 | tf_op jit(solution)/shard_map/jit(_pad)/pad | solution.py:505
  2.1 0.0 copy-done.1
  2.1 0.1 copy.9
  2.2 0.0 copy-start.2
  2.2 0.6 %copy.11.offset_ref = s32[4,8]{1,0:T(4,128)} copy(s32[4,8]{0,1:T(8,128)S(1)} %bitcast.4) | data formatting | bytes 256 | tf_op jit(solution)/shard_map/reshape | solution.py:547
  2.8 0.0 copy-done.2
  2.9 0.0 copy-start
  2.9 0.1 rev.3
  3.0 0.6 %copy-done = bf16[10,41]{1,0:T(8,128)(2,1)S(1)} copy-done((bf16[10,41]{1,0:T(8,128)(2,1)S(1)}, bf16[10,41]{1,0:T(8,128)(2,1)}, u32[]{:S(2)}) %copy-start) | copy-done | bytes 844
  3.6 0.1 slice.8
  3.6 0.7 %pad_maximum_fusion.taps_ref = f32[20,256]{1,0:T(8,128)} fusion(f32[20,4]{1,0:T(8,128)S(1)} %bitcast.3, f32[20,37]{1,0:T(8,128)S(1)} %slice.8, f32[256]{0:T(256)S(1)} %pad.9.clone), kind=kLoop, calls=%fused_computation | loop fusion | flops 10240 | bytes 24784 | tf_op jit(solution)/shard_map/concatenate | solution.py:507
  4.3 48.6 %shard_map.82 = f32[1,128,512]{2,1,0:T(8,128)} custom-call(s32[4]{0:T(128)} %exposure_ref.1, s32[4,4]{1,0:T(4,128)} %patch_ref.1, s32[4,8]{1,0:T(4,128)} %copy.11.offset_ref, f32[8,128]{1,0:T(8,128)} %fusion.6.top_ref, bf16[4,256,256]{2,1,0:T(8,128)(2,1)} %tiles_hbm.1, f32[20,256]{1,0:T(8,128)} %pad_maximum_fusion.taps_ref), custom_call_target="tpu_custom_call" | custom-call | tf_op jit(solution)/shard_map/pallas_call | solution.py:516
  53.0 1.7 %copy.13 = f32[1,128,512]{2,1,0:T(8,128)} copy(f32[1,128,512]{2,1,0:T(8,128)} %shard_map.82) | data formatting | bytes 524288
  (2 shorter events, 0.0 us)
Async XLA Ops:
  0.0 0.7 %copy-start.4 = (bf16[2]{0:T(256)(128)(2,1)S(1)}, bf16[2]{0:T(256)(128)(2,1)}, u32[]{:S(2)}) copy-start(bf16[2]{0:T(256)(128)(2,1)} %param.13) | copy-start | bytes 16
  0.8 0.7 %copy-start.3 = (bf16[2,10]{1,0:T(2,128)(2,1)S(1)}, bf16[2,10]{1,0:T(2,128)(2,1)}, u32[]{:S(2)}) copy-start(bf16[2,10]{1,0:T(2,128)(2,1)} %param.12) | copy-start | bytes 124
  0.8 1.3 %copy-start.1 = (s32[4,4,2]{1,2,0:T(2,128)S(1)}, s32[4,4,2]{1,2,0:T(2,128)}, u32[]{:S(2)}) copy-start(s32[4,4,2]{1,2,0:T(2,128)} %param.11) | copy-start | bytes 388
  2.2 0.7 %copy-start.2 = (bf16[10,41]{1,0:T(8,128)(2,1)S(1)}, bf16[10,41]{1,0:T(8,128)(2,1)}, u32[]{:S(2)}) copy-start(bf16[10,41]{1,0:T(8,128)(2,1)} %param.15) | copy-start | bytes 2464
  2.9 0.7 %copy-start = (bf16[10,41]{1,0:T(8,128)(2,1)S(1)}, bf16[10,41]{1,0:T(8,128)(2,1)}, u32[]{:S(2)}) copy-start(bf16[10,41]{1,0:T(8,128)(2,1)} %param.14) | copy-start | bytes 2464
